TPU v7x, 128 devices: a whole 4x4x4 slice. The times are simulated.
128 devices in a mesh: row: 8 (over y, core), col: 16 (over z, x).
Axes of the slice: x: 4, y: 4, z: 4, core: 2. Of those that a mesh axis runs over, the one named last changes fastest.
Arguments:
- parent_blocks: float32 [8, 2048, 2048], P('row', 'col'), as said below
- shifts: float32 [8], replicated, may hold values from -0.5 to 0.5
- orders: int32 [8], replicated, may hold values from 256 to 2048, as said below
- child_order: int32 [8], replicated, may hold values from 0 to 7, each once
Outputs:
- polar: float32 [8, 2048, 2048], P('row', 'col')
Inputs may be any that keep to these rules, and one draw needn't show every extreme that they name: `orders`: each order is a multiple of 128 from 256 to 2048; some subproblem has order 2048. `parent_blocks`: each matrix is symmetric. `child_order`: a permutation of the subproblems; slot k lies in child group k.
All inputs are finite; a program needn't handle non-finite values.
Results may differ from a plain program's by a relative error of at most 0.0001.
Values sent between devices are 32-bit elements; how exact they have to be, the bound alone decides.
A program may use at most 64 MiB of HBM per device.

v0:
```python
import jax
import jax.numpy as jnp
from jax import lax
from jax.sharding import PartitionSpec as P

STEPS = 2


def matmul_batch(left, right):
    return jnp.einsum("sik,skj->sij", left, right, precision=lax.Precision.HIGHEST)


def local(parent_blocks, shifts, orders, child_order):
    slots = parent_blocks.shape[0]
    strip = parent_blocks.shape[1]
    width = parent_blocks.shape[2]
    total_subs = orders.shape[0]
    row_idx = lax.axis_index("row")
    col_idx = lax.axis_index("col")
    slot_range = jnp.arange(slots, dtype=jnp.int32)
    own_subs = row_idx * slots + slot_range
    row_global = col_idx * strip + jnp.arange(strip, dtype=jnp.int32)
    col_global = jnp.arange(width, dtype=jnp.int32)
    limit = orders[own_subs][:, None, None]
    live = (row_global[None, :, None] < limit) & (col_global[None, None, :] < limit)
    diagonal = row_global[:, None] == col_global[None, :]
    own_shift = shifts[own_subs]
    moved = parent_blocks - jnp.where(diagonal[None], own_shift[:, None, None], jnp.float32(0.0))
    shifted = jnp.where(live, moved, jnp.float32(0.0))
    root_order = jnp.sqrt(orders.astype(jnp.float32))
    local_sums = jnp.sum(shifted * shifted, axis=(1, 2))
    match = (jnp.arange(total_subs, dtype=jnp.int32)[:, None] == own_subs[None, :]).astype(
        jnp.float32
    )
    spread = jnp.sum(match * local_sums[None, :], axis=1)
    sumsq = lax.psum(spread, ("row", "col"))
    scale_all = root_order / (2.0 * jnp.sqrt(sumsq + 1e-06))
    sending = shifted * scale_all[own_subs][:, None, None]
    everything = lax.all_gather(sending, "row", axis=0, tiled=True)
    child_own = child_order[row_idx * slots + slot_range]
    picked = everything[child_own]
    child_root = root_order[child_own]
    iterate = picked
    for step in range(STEPS):
        whole = lax.all_gather(iterate, "col", axis=1, tiled=True)
        square = matmul_batch(iterate, whole)
        cubic = matmul_batch(square, whole)
        iterate = 1.5 * iterate - 0.5 * cubic
    return iterate * child_root[:, None, None]


def solution(mesh):
    in_specs = (P("row", "col", None), P(), P(), P())
    out_specs = P("row", "col", None)
    return jax.shard_map(local, mesh=mesh, in_specs=in_specs, out_specs=out_specs, check_vma=False)
```

profile of v0, /device:TPU:1, one launch (start us, length us, event | category | flops | bytes accessed | tf_op | source)
XLA Modules:
  0.0 413.0 jit_solution(5485836694615514704)
XLA Ops:
  6.5 0.0 all-gather.5.cloned.1.call-start
  6.5 1.3 dynamic-slice.13
  7.8 0.7 broadcast_compare_fusion
  8.5 0.7 iota_compare_fusion.1
  9.2 1.3 dynamic-slice.14
  10.5 3.1 multiply_reduce_fusion
  13.7 0.6 compare_select_fusion
  14.3 68.7 %psum.7 = f32[8]{0:T(128)S(1)} all-reduce(f32[8]{0:T(128)S(1)} %compare_select_fusion), channel_id=1, replica_groups=mesh['row'=8,'col'=16] {'row','col'}, use_global_device_ids=true, to_apply=%region_1.2 | all-reduce | flops 8 | bytes 64 | tf_op jit(solution)/shard_map/psum | solution.py:36
  83.0 0.7 convert_sqrt_fusion
  83.7 0.6 dynamic-slice.15
  84.3 3.9 fusion.14
  88.2 0.0 all-gather.5.cloned.1.call-update
  88.2 0.0 all-gather.7.cloned.1.call-start
  88.3 1.3 dynamic-slice.16
  91.4 43.5 %all-gather.5.cloned.1.call-done = f32[8,128,2048]{2,1,0:T(8,128)} async-done(((f32[1,128,2048]{2,1,0:T(8,128)}), f32[8,128,2048]{2,1,0:T(8,128)}) %all-gather.5.cloned.1.call-update) | async-done | bytes 8388624 | tf_op jit(solution)/shard_map/all_gather | solution.py:39
  134.9 2.3 constant_dynamic-slice_fusion
  137.2 0.0 copy-start.3
  137.2 0.0 all-gather.7.cloned.1.call-update
  137.2 0.0 all-gather.9.cloned.1.call-start
  137.3 111.3 %all-gather.7.cloned.1.call-done = f32[1,2048,2048]{2,1,0:T(8,128)} async-done(((f32[1,128,2048]{2,1,0:T(8,128)}), f32[1,2048,2048]{2,1,0:T(8,128)}) %all-gather.7.cloned.1.call-update) | async-done | bytes 16777232 | tf_op jit(solution)/shard_map/all_gather | solution.py:45
  248.6 0.0 copy-start
  248.6 13.3 %fusion.2 = f32[128,2048]{1,0:T(8,128)S(1)} fusion(f32[1,2048,2048]{2,1,0:T(8,128)} %all-gather.7.cloned.1.call-done, f32[1,128,2048]{2,1,0:T(8,128)} %constant_dynamic-slice_fusion), kind=kOutput, calls=%fused_computation.2 | convolution fusion | flops 6442450944 | bytes 18874368 | tf_op jit(solution)/shard_map/sik,skj->sij/dot_general | solution.py:10
  261.8 0.0 copy-done.3
  261.9 0.0 copy-done
  261.9 9.9 %fusion.10 = f32[128,2048]{1,0:T(8,128)} fusion(f32[128,2048]{1,0:T(8,128)S(1)} %fusion.2, f32[1,2048,2048]{2,1,0:T(8,128)S(1)} %copy-done, f32[1,128,2048]{2,1,0:T(8,128)S(1)} %copy-done.3), kind=kOutput, calls=%fused_computation.9 | convolution fusion | flops 6443237376 | bytes 19922944 | tf_op jit(solution)/shard_map/sik,skj->sij/dot_general | solution.py:10
  271.7 0.0 copy-start.2
  271.7 0.0 all-gather.9.cloned.1.call-update
  271.8 0.6 dynamic-slice.18
  272.3 110.6 %all-gather.9.cloned.1.call-done = f32[2048,2048]{1,0:T(8,128)} async-done(((f32[128,2048]{1,0:T(8,128)}), f32[2048,2048]{1,0:T(8,128)}) %all-gather.9.cloned.1.call-update) | async-done | bytes 16777232 | tf_op jit(solution)/shard_map/all_gather | solution.py:45
  383.0 0.0 copy-start.1
  383.0 13.1 %fusion.15 = f32[128,2048]{1,0:T(8,128)S(1)} fusion(f32[128,2048]{1,0:T(8,128)} %fusion.10, f32[2048,2048]{1,0:T(8,128)} %all-gather.9.cloned.1.call-done), kind=kOutput, calls=%fused_computation.23 | convolution fusion | flops 6442450944 | bytes 18874368 | tf_op jit(solution)/shard_map/sik,skj->sij/dot_general | solution.py:10
  396.1 0.0 copy-done.2
  396.1 0.0 copy-done.1
  396.1 10.4 %fusion.6 = f32[1,128,2048]{2,1,0:T(8,128)} fusion(f32[128,2048]{1,0:T(8,128)S(1)} %fusion.15, f32[2048,2048]{1,0:T(8,128)S(1)} %copy-done.1, f32[128,2048]{1,0:T(8,128)S(1)} %copy-done.2, f32[]{:T(128)} %bitcast.8), kind=kOutput, calls=%fused_computation.7 | convolution fusion | flops 6443499520 | bytes 19922948 | tf_op jit(solution)/shard_map/sik,skj->sij/dot_general | solution.py:10
  (1 shorter events, 0.0 us)
Async XLA Ops:
  6.5 128.4 %all-gather.5.cloned.1.call-start = ((), (), s32[]{:S(2)}) async-start(), calls=%async_computation | async-start | bytes 9437184 | tf_op jit(solution)/shard_map/all_gather | solution.py:39
  88.2 160.4 %all-gather.7.cloned.1.call-start = ((), (), s32[]{:S(2)}) async-start(), calls=%async_computation.1 | async-start | bytes 17825792 | tf_op jit(solution)/shard_map/all_gather | solution.py:45
  137.2 124.6 %copy-start.3 = (f32[1,128,2048]{2,1,0:T(8,128)S(1)}, f32[1,128,2048]{2,1,0:T(8,128)}, u32[]{:S(2)}) copy-start(f32[1,128,2048]{2,1,0:T(8,128)} %constant_dynamic-slice_fusion) | copy-start | bytes 3145732
  137.2 245.7 %all-gather.9.cloned.1.call-start = ((), (), s32[]{:S(2)}) async-start(), calls=%async_computation.2 | async-start | bytes 17825792 | tf_op jit(solution)/shard_map/all_gather | solution.py:45
  248.6 13.3 %copy-start = (f32[1,2048,2048]{2,1,0:T(8,128)S(1)}, f32[1,2048,2048]{2,1,0:T(8,128)}, u32[]{:S(2)}) copy-start(f32[1,2048,2048]{2,1,0:T(8,128)} %all-gather.7.cloned.1.call-done) | copy-start | bytes 50331652
  271.7 124.3 %copy-start.2 = (f32[128,2048]{1,0:T(8,128)S(1)}, f32[128,2048]{1,0:T(8,128)}, u32[]{:S(2)}) copy-start(f32[128,2048]{1,0:T(8,128)} %fusion.10) | copy-start | bytes 3145732
  383.0 13.1 %copy-start.1 = (f32[2048,2048]{1,0:T(8,128)S(1)}, f32[2048,2048]{1,0:T(8,128)}, u32[]{:S(2)}) copy-start(f32[2048,2048]{1,0:T(8,128)} %all-gather.9.cloned.1.call-done) | copy-start | bytes 50331652
Sparse Core Ops, SparseCore 0:
  88.3 46.5 all-gather.4
  137.4 111.1 all-gather.6
  271.9 111.0 all-gather.8
where the time goes:
time: 413 us
  waiting for transfers between devices  265 us (64%)
  blocking collectives  68.7 us (17%)
  matrix products  46.7 us (11%)
  between operations  15.1 us (4%)
  other arithmetic  9.65 us (2%)
  local copies, waits for them, and re-layouts  7.38 us (2%)
    all_gather x2, waiting for transfers between devices, local(): whole = lax.all_gather(iterate, 'col', axis=1, tiled=True)  222 us
    psum x1, blocking collectives, local(): sumsq = lax.psum(spread, ('row', 'col'))  68.7 us
    dot_general x4, matrix products, matmul_batch(): jnp.einsum('sik,skj->sij', left, right, precision=lax.Precision.HIGHEST)  46.7 us
    all_gather x1, waiting for transfers between devices, local(): everything = lax.all_gather(sending, 'row', axis=0, tiled=True)  43.5 us
  transfers between devices with their start and end apart: 3, of which 3 were waited for; matrix products, arithmetic and copies ran while one was open for 0% of the time, Pallas kernels for 0%

commit v1 on v0

v1 whole, which is shorter than its diff:
```python
import jax
import jax.numpy as jnp
from jax import lax
from jax.experimental import pallas as pl
from jax.experimental.pallas import tpu as pltpu
from jax.sharding import PartitionSpec as P

MESH = pl.DeviceIdType.MESH
f32, bf16 = jnp.float32, jnp.bfloat16

SIDE = 4
STRIPS = SIDE * SIDE
ROWS = 8
B = 128
M = STRIPS * B
TILE = 1024

HALVES = ((0, 2), (2, 0), (2, 2))
CHUNKS = (
    ("x", ((0, 0), (0, 1))),
    ("z", ((2, 1),) + HALVES),
    ("x", ((1, 0), (1, 1))),
    ("z", ((1, 2), (1, 3))),
)
LINE = {"x": (0, 1), "z": (1, 0)}


def block_rows(d):
    return B // 2 if d in HALVES else B


def chunk_rows(q):
    return sum(block_rows(d) for d in CHUNKS[q][1])


def offset(q, d):
    total = 0
    for e in CHUNKS[q][1]:
        if e == d:
            return total
        total += block_rows(e)


def plus(r, e, k=1):
    return ((r[0] + k * e[0]) % SIDE, (r[1] + k * e[1]) % SIDE)


def flat(r):
    return SIDE * r[0] + r[1]


def split(v):
    high = v.astype(bf16)
    return high, (v - high.astype(f32)).astype(bf16)


def kernel(x_ref, shifts, orders, child, o_ref, *scratch):
    nq = len(CHUNKS)
    pack, parts, chosen, stage = (scratch[i * nq : (i + 1) * nq] for i in range(4))
    sh, sl, lhs, cur, first_strip, res, ssq, scale, s1, r1, s2, r2, s3, r3 = scratch[4 * nq :]

    row, col = lax.axis_index("row"), lax.axis_index("col")
    z, x = col // SIDE, lax.rem(col, SIDE)

    def place(r):
        return lax.rem(z + r[0], SIDE) * SIDE + lax.rem(x + r[1], SIDE)

    def to_row(delta):
        return {"row": lax.rem(row + delta, ROWS)}

    def to_col(e, sign):
        return {"col": place((e[0] * (1 if sign > 0 else SIDE - 1), e[1] * (1 if sign > 0 else SIDE - 1)))}

    barrier = pltpu.get_barrier_semaphore()
    for delta in range(1, ROWS):
        pl.semaphore_signal(barrier, inc=1, device_id=to_row(delta), device_id_type=MESH)
    for e in LINE.values():
        for sign in (1, -1):
            pl.semaphore_signal(barrier, inc=1, device_id=to_col(e, sign), device_id_type=MESH)

    order, shift = orders[row], shifts[row]
    eye = (
        lax.broadcasted_iota(jnp.int32, (B, B), 0) == lax.broadcasted_iota(jnp.int32, (B, B), 1)
    )
    for q in range(nq):
        for d in CHUNKS[q][1]:
            there = place(d)
            blk = x_ref[0, :, pl.ds(pl.multiple_of(there * B, B), B)]
            if d == (0, 0):
                blk = blk - jnp.where(eye, shift, jnp.float32(0.0))
            live = jnp.maximum(col, there) * B < order
            blk = blk * jnp.where(live, jnp.float32(1.0), jnp.float32(0.0))
            at = offset(q, d)
            if d in HALVES:
                leads = (x if d[0] == 0 else z) < SIDE // 2
                one = jnp.where(leads, jnp.float32(1.0), jnp.float32(0.0))
                turned = blk.T
                pack[q][at : at + B // 2] = blk[: B // 2] * one + turned[B // 2 :] * (1.0 - one)
            else:
                pack[q][at : at + B] = blk

    pl.semaphore_wait(barrier, ROWS - 1 + 4)

    first = {}
    for q in range(nq):
        n = chunk_rows(q) // ROWS
        for delta in range(1, ROWS):
            j = lax.rem(row + delta, ROWS)
            copy = pltpu.make_async_remote_copy(
                src_ref=pack[q].at[pl.ds(pl.multiple_of(j * n, 8), n)],
                dst_ref=parts[q].at[row],
                send_sem=s1.at[q * ROWS + delta],
                recv_sem=r1.at[q * ROWS + delta],
                device_id=to_row(delta),
                device_id_type=MESH,
            )
            copy.start()
            first[q, delta] = copy
        parts[q][row] = pack[q][pl.ds(pl.multiple_of(row * n, 8), n)]

    second = {}
    for q in range(nq):
        n = chunk_rows(q) // ROWS
        for delta in range(1, ROWS):
            first[q, delta].wait_recv()
        mine = pl.ds(pl.multiple_of(row * n, 8), n)
        for delta in range(1, ROWS):
            k = lax.rem(row + delta, ROWS)
            chosen[q][delta] = parts[q][child[k]]
            copy = pltpu.make_async_remote_copy(
                src_ref=chosen[q].at[delta],
                dst_ref=stage[q].at[0, mine],
                send_sem=s2.at[q * ROWS + delta],
                recv_sem=r2.at[q * ROWS + delta],
                device_id=to_row(delta),
                device_id_type=MESH,
            )
            copy.start()
            second[q, delta] = copy
        stage[q][0, mine] = parts[q][child[row]]

    third = {}

    def send(q, r, half, e, sign):
        n = chunk_rows(q)
        rows = {"all": pl.ds(0, n), "top": pl.ds(0, n // 2), "low": pl.ds(n // 2, n // 2)}[half]
        lands = plus(r, e, -sign)
        slot = (q * STRIPS + flat(lands)) * 2 + (1 if half == "low" else 0)
        copy = pltpu.make_async_remote_copy(
            src_ref=stage[q].at[flat(r), rows],
            dst_ref=stage[q].at[flat(lands), rows],
            send_sem=s3.at[slot],
            recv_sem=r3.at[slot],
            device_id=to_col(e, sign),
            device_id_type=MESH,
        )
        copy.start()
        third[q, lands, half] = copy

    def wait(q, r, half):
        third[q, r, half].wait_recv()

    def axes(q):
        a = LINE[CHUNKS[q][0]]
        return a, (a[1], a[0])

    def across(q, r):
        _, b = axes(q)
        send(q, r, "all", b, 1)
        send(q, r, "all", b, -1)

    for q in range(nq):
        a, b = axes(q)
        for delta in range(1, ROWS):
            second[q, delta].wait_recv()
        send(q, (0, 0), "all", a, 1)
        send(q, (0, 0), "all", a, -1)
        across(q, (0, 0))

    ssq[...] = jnp.zeros_like(ssq)

    def put(i, j, blk):
        at_i, at_j = pl.ds(pl.multiple_of(i * B, B), B), pl.ds(pl.multiple_of(j * B, B), B)
        high, low = split(blk)
        sh[at_i, at_j] = high
        sl[at_i, at_j] = low
        if i is not j:
            high, low = split(blk.T)
            sh[at_j, at_i] = high
            sl[at_j, at_i] = low

    def square(blk, weight):
        ssq[...] += weight * jnp.sum((blk * blk).reshape(-1, 8, B), axis=0)

    def unpack(q, k):
        a, b = axes(q)

        def body(t, _):
            rz, rx = t * a[0] + k * b[0], t * a[1] + k * b[1]
            r = rz * SIDE + rx
            for d in CHUNKS[q][1]:
                if d in HALVES:
                    continue
                at = offset(q, d)
                blk = stage[q][r, at : at + B]
                if d == (0, 0):
                    square(blk, 1.0)
                    put(r, r, blk)
                else:
                    square(blk, 2.0)
                    put(r, lax.rem(rz + d[0], SIDE) * SIDE + lax.rem(rx + d[1], SIDE), blk)
            return 0

        lax.fori_loop(0, SIDE, body, 0)

    def unpack_halves(q):
        for d in HALVES:
            at = offset(q, d)

            def body(t, _):
                if d[0] == 0:
                    rz, rx = t // 2, lax.rem(t, 2)
                    leads = lax.rem(x + rx, SIDE) < SIDE // 2
                else:
                    rz, rx = t // SIDE, lax.rem(t, SIDE)
                    leads = lax.rem(z + rz, SIDE) < SIDE // 2
                r = rz * SIDE + rx
                o = lax.rem(rz + d[0], SIDE) * SIDE + lax.rem(rx + d[1], SIDE)
                lead = jnp.where(leads, r, o)
                trail = r + o - lead
                blk = jnp.concatenate(
                    [stage[q][lead, at : at + B // 2], stage[q][trail, at : at + B // 2]], axis=0
                )
                square(blk, 2.0)
                put(lead, trail, blk)
                return 0

            lax.fori_loop(0, STRIPS // 2, body, 0)

    def line(q):
        a, b = axes(q)
        wait(q, plus((0, 0), a, -1), "all")
        send(q, plus((0, 0), a, -1), "top", a, 1)
        across(q, plus((0, 0), a, -1))
        wait(q, a, "all")
        send(q, a, "low", a, -1)
        across(q, a)

    def line_end(q):
        a, b = axes(q)
        far = plus((0, 0), a, 2)
        wait(q, far, "top")
        wait(q, far, "low")
        across(q, far)

    def near(q):
        a, b = axes(q)
        for k in (0, -1, 1, 2):
            r = plus((0, 0), a, k)
            wait(q, plus(r, b, -1), "all")
            send(q, plus(r, b, -1), "top", b, 1)
            wait(q, plus(r, b, 1), "all")
            send(q, plus(r, b, 1), "low", b, -1)

    def far(q):
        a, b = axes(q)
        for k in (0, -1, 1, 2):
            r = plus(plus((0, 0), a, k), b, 2)
            wait(q, r, "top")
            wait(q, r, "low")

    for q in range(nq):
        line(q)
    for q in range(nq):
        line_end(q)
    near(0)
    near(1)
    unpack(0, 0)
    unpack(1, 0)
    near(2)
    near(3)
    unpack(2, 0)
    unpack(3, 0)
    for q in range(nq):
        unpack(q, 1)
        unpack(q, 3)
    for q in range(nq):
        far(q)
        unpack(q, 2)
        if q == 1:
            unpack_halves(q)

    order_here = orders[child[row]]
    root = jnp.sqrt(jnp.full((1, TILE), order_here, jnp.int32).astype(f32))
    total = jnp.sum(jnp.sum(ssq[...], axis=0, keepdims=True), axis=1, keepdims=True)
    scale[...] = root / (2.0 * jnp.sqrt(jnp.broadcast_to(total, (1, TILE)) + 1e-06))

    def load(v, cs):
        high, low = split(v)
        lhs[0:B, cs] = high
        lhs[B : 2 * B, cs] = low

    tiles = M // TILE

    def cols(j):
        return pl.ds(pl.multiple_of(j * TILE, TILE), TILE)

    def begin(j, _):
        cs = cols(j)
        v = (sh[0:B, cs].astype(f32) + sl[0:B, cs].astype(f32)) * scale[...]
        first_strip[:, cs] = v
        load(v, cs)
        return 0

    lax.fori_loop(0, tiles, begin, 0)

    def apply(j, _):
        cs = cols(j)
        both = jnp.dot(lhs[...], sh[:, cs], preferred_element_type=f32)
        low = jnp.dot(lhs[0:B], sl[:, cs], preferred_element_type=f32)
        cur[:, cs] = (both[0:B] + both[B : 2 * B] + low) * scale[...]
        return 0

    def reload(j, _):
        load(cur[:, cols(j)], cols(j))
        return 0

    def twice(m, _):
        lax.fori_loop(0, tiles, apply, 0)
        lax.fori_loop(0, tiles, reload, 0)
        lax.fori_loop(0, tiles, apply, 0)
        is_first = m == 0
        weight = jnp.where(
            m == 1, jnp.float32(-1.125), jnp.where(m == 2, jnp.float32(0.75), jnp.float32(-0.125))
        )

        @pl.when(is_first)
        def _():
            def step(j, _):
                cs = cols(j)
                v = 1.5 * first_strip[:, cs] - 0.5 * cur[:, cs]
                res[:, cs] = 1.5 * v
                load(v, cs)
                return 0

            lax.fori_loop(0, tiles, step, 0)

        @pl.when(jnp.logical_not(is_first))
        def _():
            def step(j, _):
                cs = cols(j)
                v = cur[:, cs]
                res[:, cs] += weight * v
                load(v, cs)
                return 0

            lax.fori_loop(0, tiles, step, 0)

        return 0

    lax.fori_loop(0, 4, twice, 0)

    for rz in range(SIDE):
        for rx in range(SIDE):
            r = flat((rz, rx))
            o_ref[0, :, pl.ds(pl.multiple_of(place((rz, rx)) * B, B), B)] = (
                res[:, r * B : (r + 1) * B] * root[:, 0:B]
            )

    for copies in (first, second, third):
        for copy in copies.values():
            copy.wait_send()


def local(parent_blocks, shifts, orders, child_order):
    nq = len(CHUNKS)
    rows = [chunk_rows(q) for q in range(nq)]
    smem = pl.BlockSpec(memory_space=pltpu.SMEM)
    vmem = pl.BlockSpec(memory_space=pltpu.VMEM)
    return pl.pallas_call(
        kernel,
        out_shape=jax.ShapeDtypeStruct(parent_blocks.shape, f32),
        in_specs=[vmem, smem, smem, smem],
        out_specs=vmem,
        scratch_shapes=[pltpu.VMEM((n, B), f32) for n in rows]
        + [pltpu.VMEM((ROWS, n // ROWS, B), f32) for n in rows]
        + [pltpu.VMEM((ROWS, n // ROWS, B), f32) for n in rows]
        + [pltpu.VMEM((STRIPS, n, B), f32) for n in rows]
        + [
            pltpu.VMEM((M, M), bf16),
            pltpu.VMEM((M, M), bf16),
            pltpu.VMEM((2 * B, M), bf16),
            pltpu.VMEM((B, M), f32),
            pltpu.VMEM((B, M), f32),
            pltpu.VMEM((B, M), f32),
            pltpu.VMEM((8, B), f32),
            pltpu.VMEM((1, TILE), f32),
            pltpu.SemaphoreType.DMA((nq * ROWS,)),
            pltpu.SemaphoreType.DMA((nq * ROWS,)),
            pltpu.SemaphoreType.DMA((nq * ROWS,)),
            pltpu.SemaphoreType.DMA((nq * ROWS,)),
            pltpu.SemaphoreType.DMA((nq * STRIPS * 2,)),
            pltpu.SemaphoreType.DMA((nq * STRIPS * 2,)),
        ],
        compiler_params=pltpu.CompilerParams(
            collective_id=0, has_side_effects=True, vmem_limit_bytes=48 * 2**20
        ),
        cost_estimate=pl.CostEstimate(
            flops=8 * 3 * 2 * B * M * M, bytes_accessed=2 * 4 * B * M, transcendentals=0
        ),
        name="sign_steps",
    )(parent_blocks, shifts, orders, child_order)


def solution(mesh):
    in_specs = (P("row", "col", None), P(), P(), P())
    out_specs = P("row", "col", None)
    return jax.shard_map(local, mesh=mesh, in_specs=in_specs, out_specs=out_specs, check_vma=False)
```

time: 413 us -> 106 us (0.26)
  waiting for transfers between devices: 265 us -> 0 us
  Pallas kernels: 0 us -> 102 us
  blocking collectives: 68.7 us -> 0 us
  matrix products: 46.7 us -> 0 us
  between operations: 15.1 us -> 0.01 us
  other arithmetic: 9.65 us -> 0 us
    all_gather x3 -> x0, waiting for transfers between devices: 265 us -> none  [the longest x2 222 us: local(): whole = lax.all_gather(iterate, 'col', axis=1, tiled=True)]
    pallas_call x0 -> x1, Pallas kernels: none -> 102 us  [local(): pl.pallas_call(kernel, out_shape=jax.ShapeDtypeStruct(parent_blocks.shape...]
    psum x1 -> x0, blocking collectives: 68.7 us -> none  [local(): sumsq = lax.psum(spread, ('row', 'col'))]
    dot_general x4 -> x0, matrix products: 46.7 us -> none  [matmul_batch(): jnp.einsum('sik,skj->sij', left, right, precision=lax.Precision.HIGHEST)]
    gather x6 -> x0, local copies, waits for them, and re-layouts: 7.37 us -> none  [the longest x1 2.29 us: local(): picked = everything[child_own]]
    mul x2 -> x0, other arithmetic: 4.5 us -> none  [the longest x1 3.87 us: local(): sending = shifted * scale_all[own_subs][:, None, None]]
    unnamed x8 -> x9, local copies, waits for them, and re-layouts: 0.02 us -> 4.16 us
  transfers between devices with their start and end apart: 3 -> 0, of which waited for: 3 -> 0; matrix products, arithmetic and copies ran while one was open for 0% -> 0% of each run, Pallas kernels for 0% -> 0%
where the time goes in v1:
time: 106 us
  Pallas kernels  102 us (96%)
  local copies, waits for them, and re-layouts  4.16 us (4%)
    pallas_call x1, Pallas kernels, local(): pl.pallas_call(kernel, out_shape=jax.ShapeDtypeStruct(parent_blocks.shape...  102 us
    unnamed x9, local copies, waits for them, and re-layouts  4.16 us

profile of v1, /device:TPU:1, one launch (start us, length us, event | category | flops | bytes accessed | tf_op | source)
XLA Modules:
  0.0 106.3 jit_solution(6087994696399769763)
XLA Ops:
  0.0 0.0 copy-start
  0.0 1.2 %copy-done = f32[1,128,2048]{2,1,0:T(8,128)S(1)} copy-done((f32[1,128,2048]{2,1,0:T(8,128)S(1)}, f32[1,128,2048]{2,1,0:T(8,128)}, u32[]{:S(2)}) %copy-start) | copy-done | bytes 1048600
  1.2 0.0 copy-start.1
  1.2 0.7 copy-done.1
  1.9 0.0 copy-start.2
  1.9 0.7 copy-done.2
  2.5 0.0 copy-start.3
  2.5 0.7 copy-done.3
  3.2 102.1 %sign_steps.1 = f32[1,128,2048]{2,1,0:T(8,128)S(1)} custom-call(f32[1,128,2048]{2,1,0:T(8,128)S(1)} %copy-done, f32[8]{0:T(128)S(1)} %copy-done.1, s32[8]{0:T(128)S(1)} %copy-done.2, s32[8]{0:T(128)S(1)} %copy-done.3), custom_call_target="tpu_custom_call" | custom-call | flops 25769803776 | bytes 2097152 | tf_op jit(solution)/shard_map/sign_steps/pallas_call | solution.py:380
  105.3 1.0 copy.6
Async XLA Ops:
  0.0 1.2 %copy-start = (f32[1,128,2048]{2,1,0:T(8,128)S(1)}, f32[1,128,2048]{2,1,0:T(8,128)}, u32[]{:S(2)}) copy-start(f32[1,128,2048]{2,1,0:T(8,128)} %x_ref.1) | copy-start | bytes 3145732
  1.2 0.7 copy-start.1
  1.9 0.7 copy-start.2
  2.5 0.7 copy-start.3

commit v2 on v1

--- a/solution.py
+++ b/solution.py
@@ -13,7 +13,6 @@
 ROWS = 8
 B = 128
 M = STRIPS * B
-TILE = 1024
 
 HALVES = ((0, 2), (2, 0), (2, 2))
 CHUNKS = (
@@ -54,10 +53,20 @@
     return high, (v - high.astype(f32)).astype(bf16)
 
 
-def kernel(x_ref, shifts, orders, child, o_ref, *scratch):
+def kernel(x_hbm, shifts_hbm, orders_hbm, child_hbm, o_ref, *scratch):
     nq = len(CHUNKS)
     pack, parts, chosen, stage = (scratch[i * nq : (i + 1) * nq] for i in range(4))
-    sh, sl, lhs, cur, first_strip, res, ssq, scale, s1, r1, s2, r2, s3, r3 = scratch[4 * nq :]
+    sh, sl, lhs, first_strip, res, ssq, scale, s1, r1, s2, r2, s3, r3 = scratch[4 * nq : 4 * nq + 13]
+    x_ref, shifts, orders, child, arg_sems = scratch[4 * nq + 13 :]
+
+    fetches = [
+        pltpu.make_async_copy(src, dst, arg_sems.at[i])
+        for i, (src, dst) in enumerate(
+            ((x_hbm, x_ref), (shifts_hbm, shifts), (orders_hbm, orders), (child_hbm, child))
+        )
+    ]
+    for fetch in fetches:
+        fetch.start()
 
     row, col = lax.axis_index("row"), lax.axis_index("col")
     z, x = col // SIDE, lax.rem(col, SIDE)
@@ -78,11 +87,15 @@
         for sign in (1, -1):
             pl.semaphore_signal(barrier, inc=1, device_id=to_col(e, sign), device_id_type=MESH)
 
+    for fetch in fetches:
+        fetch.wait()
+
     order, shift = orders[row], shifts[row]
     eye = (
         lax.broadcasted_iota(jnp.int32, (B, B), 0) == lax.broadcasted_iota(jnp.int32, (B, B), 1)
     )
-    for q in range(nq):
+
+    def fill(q):
         for d in CHUNKS[q][1]:
             there = place(d)
             blk = x_ref[0, :, pl.ds(pl.multiple_of(there * B, B), B)]
@@ -99,10 +112,9 @@
             else:
                 pack[q][at : at + B] = blk
 
-    pl.semaphore_wait(barrier, ROWS - 1 + 4)
-
-    first = {}
-    for q in range(nq):
+    first, second = {}, {}
+
+    def spread(q):
         n = chunk_rows(q) // ROWS
         for delta in range(1, ROWS):
             j = lax.rem(row + delta, ROWS)
@@ -118,8 +130,7 @@
             first[q, delta] = copy
         parts[q][row] = pack[q][pl.ds(pl.multiple_of(row * n, 8), n)]
 
-    second = {}
-    for q in range(nq):
+    def choose(q):
         n = chunk_rows(q) // ROWS
         for delta in range(1, ROWS):
             first[q, delta].wait_recv()
@@ -169,7 +180,7 @@
         send(q, r, "all", b, 1)
         send(q, r, "all", b, -1)
 
-    for q in range(nq):
+    def begin_gather(q):
         a, b = axes(q)
         for delta in range(1, ROWS):
             second[q, delta].wait_recv()
@@ -269,6 +280,23 @@
             wait(q, r, "top")
             wait(q, r, "low")
 
+    fill(0)
+    fill(1)
+    pl.semaphore_wait(barrier, ROWS - 1 + 4)
+    spread(0)
+    spread(1)
+    fill(2)
+    fill(3)
+    choose(0)
+    spread(2)
+    choose(1)
+    spread(3)
+    begin_gather(0)
+    begin_gather(1)
+    choose(2)
+    choose(3)
+    begin_gather(2)
+    begin_gather(3)
     for q in range(nq):
         line(q)
     for q in range(nq):
@@ -291,71 +319,40 @@
             unpack_halves(q)
 
     order_here = orders[child[row]]
-    root = jnp.sqrt(jnp.full((1, TILE), order_here, jnp.int32).astype(f32))
+    root = jnp.sqrt(jnp.full((1, M), order_here, jnp.int32).astype(f32))
     total = jnp.sum(jnp.sum(ssq[...], axis=0, keepdims=True), axis=1, keepdims=True)
-    scale[...] = root / (2.0 * jnp.sqrt(jnp.broadcast_to(total, (1, TILE)) + 1e-06))
-
-    def load(v, cs):
+    scale[...] = root / (2.0 * jnp.sqrt(jnp.broadcast_to(total, (1, M)) + 1e-06))
+
+    def load(k, v):
         high, low = split(v)
-        lhs[0:B, cs] = high
-        lhs[B : 2 * B, cs] = low
-
-    tiles = M // TILE
-
-    def cols(j):
-        return pl.ds(pl.multiple_of(j * TILE, TILE), TILE)
-
-    def begin(j, _):
-        cs = cols(j)
-        v = (sh[0:B, cs].astype(f32) + sl[0:B, cs].astype(f32)) * scale[...]
-        first_strip[:, cs] = v
-        load(v, cs)
-        return 0
-
-    lax.fori_loop(0, tiles, begin, 0)
-
-    def apply(j, _):
-        cs = cols(j)
-        both = jnp.dot(lhs[...], sh[:, cs], preferred_element_type=f32)
-        low = jnp.dot(lhs[0:B], sl[:, cs], preferred_element_type=f32)
-        cur[:, cs] = (both[0:B] + both[B : 2 * B] + low) * scale[...]
-        return 0
-
-    def reload(j, _):
-        load(cur[:, cols(j)], cols(j))
-        return 0
+        lhs[k, 0:B] = high
+        lhs[k, B : 2 * B] = low
+
+    def product(k):
+        both = jnp.dot(lhs[k], sh[...], preferred_element_type=f32)
+        low = jnp.dot(lhs[k, 0:B], sl[...], preferred_element_type=f32)
+        return (both[0:B] + both[B : 2 * B] + low) * scale[...]
+
+    own = (sh[0:B].astype(f32) + sl[0:B].astype(f32)) * scale[...]
+    first_strip[...] = own
+    res[...] = jnp.zeros_like(res)
+    load(0, own)
 
     def twice(m, _):
-        lax.fori_loop(0, tiles, apply, 0)
-        lax.fori_loop(0, tiles, reload, 0)
-        lax.fori_loop(0, tiles, apply, 0)
-        is_first = m == 0
+        begins = m == 0
+        keep = jnp.where(begins, jnp.float32(1.5), jnp.float32(0.0))
+        take = jnp.where(begins, jnp.float32(-0.5), jnp.float32(1.0))
         weight = jnp.where(
-            m == 1, jnp.float32(-1.125), jnp.where(m == 2, jnp.float32(0.75), jnp.float32(-0.125))
+            begins,
+            jnp.float32(1.5),
+            jnp.where(
+                m == 1, jnp.float32(-1.125), jnp.where(m == 2, jnp.float32(0.75), jnp.float32(-0.125))
+            ),
         )
-
-        @pl.when(is_first)
-        def _():
-            def step(j, _):
-                cs = cols(j)
-                v = 1.5 * first_strip[:, cs] - 0.5 * cur[:, cs]
-                res[:, cs] = 1.5 * v
-                load(v, cs)
-                return 0
-
-            lax.fori_loop(0, tiles, step, 0)
-
-        @pl.when(jnp.logical_not(is_first))
-        def _():
-            def step(j, _):
-                cs = cols(j)
-                v = cur[:, cs]
-                res[:, cs] += weight * v
-                load(v, cs)
-                return 0
-
-            lax.fori_loop(0, tiles, step, 0)
-
+        load(1, product(0))
+        v = keep * first_strip[...] + take * product(1)
+        res[...] += weight * v
+        load(0, v)
         return 0
 
     lax.fori_loop(0, 4, twice, 0)
@@ -375,13 +372,12 @@
 def local(parent_blocks, shifts, orders, child_order):
     nq = len(CHUNKS)
     rows = [chunk_rows(q) for q in range(nq)]
-    smem = pl.BlockSpec(memory_space=pltpu.SMEM)
-    vmem = pl.BlockSpec(memory_space=pltpu.VMEM)
+    anywhere = pl.BlockSpec(memory_space=pl.ANY)
     return pl.pallas_call(
         kernel,
         out_shape=jax.ShapeDtypeStruct(parent_blocks.shape, f32),
-        in_specs=[vmem, smem, smem, smem],
-        out_specs=vmem,
+        in_specs=[anywhere] * 4,
+        out_specs=pl.BlockSpec(memory_space=pltpu.VMEM),
         scratch_shapes=[pltpu.VMEM((n, B), f32) for n in rows]
         + [pltpu.VMEM((ROWS, n // ROWS, B), f32) for n in rows]
         + [pltpu.VMEM((ROWS, n // ROWS, B), f32) for n in rows]
@@ -389,21 +385,25 @@
         + [
             pltpu.VMEM((M, M), bf16),
             pltpu.VMEM((M, M), bf16),
-            pltpu.VMEM((2 * B, M), bf16),
-            pltpu.VMEM((B, M), f32),
+            pltpu.VMEM((2, 2 * B, M), bf16),
             pltpu.VMEM((B, M), f32),
             pltpu.VMEM((B, M), f32),
             pltpu.VMEM((8, B), f32),
-            pltpu.VMEM((1, TILE), f32),
+            pltpu.VMEM((1, M), f32),
             pltpu.SemaphoreType.DMA((nq * ROWS,)),
             pltpu.SemaphoreType.DMA((nq * ROWS,)),
             pltpu.SemaphoreType.DMA((nq * ROWS,)),
             pltpu.SemaphoreType.DMA((nq * ROWS,)),
             pltpu.SemaphoreType.DMA((nq * STRIPS * 2,)),
             pltpu.SemaphoreType.DMA((nq * STRIPS * 2,)),
+            pltpu.VMEM(parent_blocks.shape, f32),
+            pltpu.SMEM(shifts.shape, f32),
+            pltpu.SMEM(orders.shape, jnp.int32),
+            pltpu.SMEM(child_order.shape, jnp.int32),
+            pltpu.SemaphoreType.DMA((4,)),
         ],
         compiler_params=pltpu.CompilerParams(
-            collective_id=0, has_side_effects=True, vmem_limit_bytes=48 * 2**20
+            collective_id=0, has_side_effects=True, vmem_limit_bytes=60 * 2**20
         ),
         cost_estimate=pl.CostEstimate(
             flops=8 * 3 * 2 * B * M * M, bytes_accessed=2 * 4 * B * M, transcendentals=0

time: 106 us -> 102 us (0.962)
  Pallas kernels: 102 us -> 99.9 us
  local copies, waits for them, and re-layouts: 4.16 us -> 2.3 us
    pallas_call x1, Pallas kernels: 102 us -> 99.9 us  [local(): pl.pallas_call(kernel, out_shape=jax.ShapeDtypeStruct(parent_blocks.shape...]
    unnamed x9 -> x1, local copies, waits for them, and re-layouts: 4.16 us -> 2.3 us
where the time goes in v2:
time: 102 us
  Pallas kernels  99.9 us (98%)
  local copies, waits for them, and re-layouts  2.3 us (2%)
    pallas_call x1, Pallas kernels, local(): pl.pallas_call(kernel, out_shape=jax.ShapeDtypeStruct(parent_blocks.shape...  99.9 us
    unnamed x1, local copies, waits for them, and re-layouts  2.3 us

profile of v2, /device:TPU:1, one launch (start us, length us, event | category | flops | bytes accessed | tf_op | source)
XLA Modules:
  0.0 102.2 jit_solution(13904305058169021867)
XLA Ops:
  0.0 99.9 %sign_steps.1 = f32[1,128,2048]{2,1,0:T(8,128)} custom-call(f32[1,128,2048]{2,1,0:T(8,128)} %x_hbm.1, f32[8]{0:T(128)} %shifts_hbm.1, s32[8]{0:T(128)} %orders_hbm.1, s32[8]{0:T(128)} %child_hbm.1), custom_call_target="tpu_custom_call" | custom-call | flops 25769803776 | bytes 2097152 | tf_op jit(solution)/shard_map/sign_steps/pallas_call | solution.py:376
  99.9 2.3 %copy.6 = f32[1,128,2048]{2,1,0:T(8,128)} copy(f32[1,128,2048]{2,1,0:T(8,128)} %sign_steps.1) | data formatting | bytes 2097152

commit v3 on v2

--- a/solution.py
+++ b/solution.py
@@ -20,6 +20,22 @@
     ("z", ((2, 1),) + HALVES),
     ("x", ((1, 0), (1, 1))),
     ("z", ((1, 2), (1, 3))),
+)
+ORDER = (
+    ("fill", 3), ("spread", 3), ("fill", 2), ("spread", 2), ("fill", 1), ("fill", 0), ("spread", 1), ("choose", 3),
+    ("choose", 2), ("choose", 1), ("begin", 3), ("spread", 0), ("begin", 2), ("begin", 1), ("choose", 0),
+    ("lineA", 2), ("lineB", 2), ("lineB", 3), ("lineB", 1), ("line_end", 2), ("begin", 0), ("lineA", 1), ("lineA", 3),
+    ("unpack", 2, 0), ("lineA", 0), ("near", 1, -1, -1), ("line_end", 1), ("lineB", 0), ("near", 1, -1, 1),
+    ("near", 1, 1, 1), ("near", 0, 0, -1), ("near", 2, 0, -1), ("near", 0, -1, -1), ("near", 1, 0, 1),
+    ("near", 2, -1, 1), ("near", 2, 1, 1), ("line_end", 3), ("near", 1, 2, 1), ("near", 1, 1, -1), ("near", 2, 2, 1),
+    ("line_end", 0), ("near", 1, 0, -1), ("unpack", 3, 0), ("unpack", 1, 0), ("near", 3, 0, -1), ("near", 0, 1, 1),
+    ("near", 2, 1, -1), ("near", 0, -1, 1), ("near", 2, -1, -1), ("unpack", 1, 1), ("near", 3, -1, 1),
+    ("near", 2, 0, 1), ("near", 2, 2, -1), ("near", 1, 2, -1), ("near", 3, -1, -1), ("unpack", 1, 3),
+    ("unpack", 0, 0), ("near", 3, 1, 1), ("halves", 1), ("near", 3, 0, 1), ("near", 3, 1, -1), ("near", 0, 1, -1),
+    ("near", 3, 2, -1), ("near", 0, 0, 1), ("near", 0, 2, -1), ("near", 3, 2, 1), ("unpack", 2, 3), ("near", 0, 2, 1),
+    ("unpack", 0, 3), ("unpack", 2, 1), ("unpack", 3, 1), ("unpack", 0, 1), ("unpack", 3, 3), ("far", 1),
+    ("unpack", 1, 2), ("far", 2), ("halves", 2), ("unpack", 2, 2), ("far", 0), ("far", 3), ("unpack", 3, 2),
+    ("unpack", 0, 2),
 )
 LINE = {"x": (0, 1), "z": (1, 0)}
 
@@ -69,10 +85,13 @@
         fetch.start()
 
     row, col = lax.axis_index("row"), lax.axis_index("col")
-    z, x = col // SIDE, lax.rem(col, SIDE)
+    turned = lax.rem(row, 2)
+    step_z, step_x = SIDE - (SIDE - 1) * turned, 1 + (SIDE - 1) * turned
+    z, x = lax.rem(col // step_z, SIDE), lax.rem(col // step_x, SIDE)
+    true_z, true_x = col // SIDE, lax.rem(col, SIDE)
 
     def place(r):
-        return lax.rem(z + r[0], SIDE) * SIDE + lax.rem(x + r[1], SIDE)
+        return lax.rem(z + r[0], SIDE) * step_z + lax.rem(x + r[1], SIDE) * step_x
 
     def to_row(delta):
         return {"row": lax.rem(row + delta, ROWS)}
@@ -97,7 +116,7 @@
 
     def fill(q):
         for d in CHUNKS[q][1]:
-            there = place(d)
+            there = lax.rem(true_z + d[0], SIDE) * SIDE + lax.rem(true_x + d[1], SIDE)
             blk = x_ref[0, :, pl.ds(pl.multiple_of(there * B, B), B)]
             if d == (0, 0):
                 blk = blk - jnp.where(eye, shift, jnp.float32(0.0))
@@ -105,10 +124,10 @@
             blk = blk * jnp.where(live, jnp.float32(1.0), jnp.float32(0.0))
             at = offset(q, d)
             if d in HALVES:
-                leads = (x if d[0] == 0 else z) < SIDE // 2
+                leads = (true_x if d[0] == 0 else true_z) < SIDE // 2
                 one = jnp.where(leads, jnp.float32(1.0), jnp.float32(0.0))
-                turned = blk.T
-                pack[q][at : at + B // 2] = blk[: B // 2] * one + turned[B // 2 :] * (1.0 - one)
+                mirror = blk.T
+                pack[q][at : at + B // 2] = blk[: B // 2] * one + mirror[B // 2 :] * (1.0 - one)
             else:
                 pack[q][at : at + B] = blk
 
@@ -204,6 +223,8 @@
         ssq[...] += weight * jnp.sum((blk * blk).reshape(-1, 8, B), axis=0)
 
     def unpack(q, k):
+        if all(d in HALVES for d in CHUNKS[q][1]):
+            return
         a, b = axes(q)
 
         def body(t, _):
@@ -219,40 +240,52 @@
                     put(r, r, blk)
                 else:
                     square(blk, 2.0)
-                    put(r, lax.rem(rz + d[0], SIDE) * SIDE + lax.rem(rx + d[1], SIDE), blk)
+                    dz, dx = d[0] + (d[1] - d[0]) * turned, d[1] + (d[0] - d[1]) * turned
+                    put(r, lax.rem(rz + dz, SIDE) * SIDE + lax.rem(rx + dx, SIDE), blk)
             return 0
 
         lax.fori_loop(0, SIDE, body, 0)
 
-    def unpack_halves(q):
+    def unpack_halves(q, early):
+        pairs = {
+            (0, 2): ((4, 1, 1, 1),) if early else ((4, 1, 1, 0),),
+            (2, 0): ((4, 2, 1, 0), (2, 1, 1, 3)) if early else ((2, 1, 1, 2),),
+            (2, 2): ((4, 2, 2, 1),) if early else ((4, 2, 2, 0),),
+        }
         for d in HALVES:
-            at = offset(q, d)
-
-            def body(t, _):
-                if d[0] == 0:
-                    rz, rx = t // 2, lax.rem(t, 2)
-                    leads = lax.rem(x + rx, SIDE) < SIDE // 2
-                else:
-                    rz, rx = t // SIDE, lax.rem(t, SIDE)
-                    leads = lax.rem(z + rz, SIDE) < SIDE // 2
-                r = rz * SIDE + rx
-                o = lax.rem(rz + d[0], SIDE) * SIDE + lax.rem(rx + d[1], SIDE)
-                lead = jnp.where(leads, r, o)
-                trail = r + o - lead
-                blk = jnp.concatenate(
-                    [stage[q][lead, at : at + B // 2], stage[q][trail, at : at + B // 2]], axis=0
-                )
-                square(blk, 2.0)
-                put(lead, trail, blk)
-                return 0
-
-            lax.fori_loop(0, STRIPS // 2, body, 0)
-
-    def line(q):
+            at = offset(q, d) + (offset(q, d[::-1]) - offset(q, d)) * turned
+            half = pl.ds(pl.multiple_of(at, B // 2), B // 2)
+            for count, per, step, start in pairs[d]:
+
+                def body(t, _):
+                    rz, rx = t // per, lax.rem(t, per) * step + start
+                    if d[0] == 0:
+                        leads = lax.rem(x + rx, SIDE) < SIDE // 2
+                    elif d[1] == 0:
+                        leads = lax.rem(z + rz, SIDE) < SIDE // 2
+                    else:
+                        leads = lax.rem(z + rz + (x + rx - z - rz) * turned, SIDE) < SIDE // 2
+                    r = rz * SIDE + rx
+                    o = lax.rem(rz + d[0], SIDE) * SIDE + lax.rem(rx + d[1], SIDE)
+                    lead = jnp.where(leads, r, o)
+                    trail = r + o - lead
+                    blk = jnp.concatenate(
+                        [stage[q][lead, half], stage[q][trail, half]], axis=0
+                    )
+                    square(blk, 2.0)
+                    put(lead, trail, blk)
+                    return 0
+
+                lax.fori_loop(0, count, body, 0)
+
+    def line_a(q):
         a, b = axes(q)
         wait(q, plus((0, 0), a, -1), "all")
         send(q, plus((0, 0), a, -1), "top", a, 1)
         across(q, plus((0, 0), a, -1))
+
+    def line_b(q):
+        a, b = axes(q)
         wait(q, a, "all")
         send(q, a, "low", a, -1)
         across(q, a)
@@ -264,14 +297,11 @@
         wait(q, far, "low")
         across(q, far)
 
-    def near(q):
-        a, b = axes(q)
-        for k in (0, -1, 1, 2):
-            r = plus((0, 0), a, k)
-            wait(q, plus(r, b, -1), "all")
-            send(q, plus(r, b, -1), "top", b, 1)
-            wait(q, plus(r, b, 1), "all")
-            send(q, plus(r, b, 1), "low", b, -1)
+    def near(q, k, side):
+        a, b = axes(q)
+        r = plus(plus((0, 0), a, k), b, side)
+        wait(q, r, "all")
+        send(q, r, "top" if side < 0 else "low", b, -side)
 
     def far(q):
         a, b = axes(q)
@@ -280,43 +310,25 @@
             wait(q, r, "top")
             wait(q, r, "low")
 
-    fill(0)
-    fill(1)
-    pl.semaphore_wait(barrier, ROWS - 1 + 4)
-    spread(0)
-    spread(1)
-    fill(2)
-    fill(3)
-    choose(0)
-    spread(2)
-    choose(1)
-    spread(3)
-    begin_gather(0)
-    begin_gather(1)
-    choose(2)
-    choose(3)
-    begin_gather(2)
-    begin_gather(3)
-    for q in range(nq):
-        line(q)
-    for q in range(nq):
-        line_end(q)
-    near(0)
-    near(1)
-    unpack(0, 0)
-    unpack(1, 0)
-    near(2)
-    near(3)
-    unpack(2, 0)
-    unpack(3, 0)
-    for q in range(nq):
-        unpack(q, 1)
-        unpack(q, 3)
-    for q in range(nq):
-        far(q)
-        unpack(q, 2)
-        if q == 1:
-            unpack_halves(q)
+    steps = {
+        "fill": fill,
+        "spread": spread,
+        "choose": choose,
+        "begin": begin_gather,
+        "lineA": line_a,
+        "lineB": line_b,
+        "line_end": line_end,
+        "near": near,
+        "far": far,
+        "unpack": unpack,
+        "halves": lambda i: unpack_halves(1, i == 1),
+    }
+    entered = False
+    for name, *args in ORDER:
+        if name == "spread" and not entered:
+            pl.semaphore_wait(barrier, ROWS - 1 + 4)
+            entered = True
+        steps[name](*args)
 
     order_here = orders[child[row]]
     root = jnp.sqrt(jnp.full((1, M), order_here, jnp.int32).astype(f32))

time: 102 us -> 100 us (0.980)
  Pallas kernels: 99.9 us -> 97.8 us
    pallas_call x1, Pallas kernels: 99.9 us -> 97.8 us  [local(): pl.pallas_call(kernel, out_shape=jax.ShapeDtypeStruct(parent_blocks.shape...]
where the time goes in v3:
time: 100 us
  Pallas kernels  97.8 us (98%)
  local copies, waits for them, and re-layouts  2.3 us (2%)
    pallas_call x1, Pallas kernels, local(): pl.pallas_call(kernel, out_shape=jax.ShapeDtypeStruct(parent_blocks.shape...  97.8 us
    unnamed x1, local copies, waits for them, and re-layouts  2.3 us

profile of v3, /device:TPU:1, one launch (start us, length us, event | category | flops | bytes accessed | tf_op | source)
XLA Modules:
  0.0 100.1 jit_solution(3511078059767494859)
XLA Ops:
  0.0 97.8 %sign_steps.1 = f32[1,128,2048]{2,1,0:T(8,128)} custom-call(f32[1,128,2048]{2,1,0:T(8,128)} %x_hbm.1, f32[8]{0:T(128)} %shifts_hbm.1, s32[8]{0:T(128)} %orders_hbm.1, s32[8]{0:T(128)} %child_hbm.1), custom_call_target="tpu_custom_call" | custom-call | flops 25769803776 | bytes 2097152 | tf_op jit(solution)/shard_map/sign_steps/pallas_call | solution.py:388
  97.8 2.3 %copy.6 = f32[1,128,2048]{2,1,0:T(8,128)} copy(f32[1,128,2048]{2,1,0:T(8,128)} %sign_steps.1) | data formatting | bytes 2097152

commit v4 on v3

--- a/solution.py
+++ b/solution.py
@@ -13,6 +13,7 @@
 ROWS = 8
 B = 128
 M = STRIPS * B
+SPAN = M // SIDE
 
 HALVES = ((0, 2), (2, 0), (2, 2))
 CHUNKS = (
@@ -22,30 +23,38 @@
     ("z", ((1, 2), (1, 3))),
 )
 ORDER = (
-    ("fill", 3), ("spread", 3), ("fill", 2), ("spread", 2), ("fill", 1), ("fill", 0), ("spread", 1), ("choose", 3),
-    ("choose", 2), ("choose", 1), ("begin", 3), ("spread", 0), ("begin", 2), ("begin", 1), ("choose", 0),
-    ("lineA", 2), ("lineB", 2), ("lineB", 3), ("lineB", 1), ("line_end", 2), ("begin", 0), ("lineA", 1), ("lineA", 3),
-    ("unpack", 2, 0), ("lineA", 0), ("near", 1, -1, -1), ("line_end", 1), ("lineB", 0), ("near", 1, -1, 1),
-    ("near", 1, 1, 1), ("near", 0, 0, -1), ("near", 2, 0, -1), ("near", 0, -1, -1), ("near", 1, 0, 1),
-    ("near", 2, -1, 1), ("near", 2, 1, 1), ("line_end", 3), ("near", 1, 2, 1), ("near", 1, 1, -1), ("near", 2, 2, 1),
-    ("line_end", 0), ("near", 1, 0, -1), ("unpack", 3, 0), ("unpack", 1, 0), ("near", 3, 0, -1), ("near", 0, 1, 1),
-    ("near", 2, 1, -1), ("near", 0, -1, 1), ("near", 2, -1, -1), ("unpack", 1, 1), ("near", 3, -1, 1),
-    ("near", 2, 0, 1), ("near", 2, 2, -1), ("near", 1, 2, -1), ("near", 3, -1, -1), ("unpack", 1, 3),
-    ("unpack", 0, 0), ("near", 3, 1, 1), ("halves", 1), ("near", 3, 0, 1), ("near", 3, 1, -1), ("near", 0, 1, -1),
-    ("near", 3, 2, -1), ("near", 0, 0, 1), ("near", 0, 2, -1), ("near", 3, 2, 1), ("unpack", 2, 3), ("near", 0, 2, 1),
-    ("unpack", 0, 3), ("unpack", 2, 1), ("unpack", 3, 1), ("unpack", 0, 1), ("unpack", 3, 3), ("far", 1),
-    ("unpack", 1, 2), ("far", 2), ("halves", 2), ("unpack", 2, 2), ("far", 0), ("far", 3), ("unpack", 3, 2),
-    ("unpack", 0, 2),
+    ("fill", 3), ("spread", 3), ("fill", 1), ("fill", 2), ("spread", 2), ("spread", 1), ("choose", 3), ("choose", 2),
+    ("choose", 1), ("begin", 3), ("fill", 0), ("spread", 0), ("begin", 2), ("begin", 1), ("lineB", 3), ("choose", 0),
+    ("lineA", 3), ("lineB", 2), ("lineB", 1), ("extra", 0), ("lineA", 2), ("take", 0), ("begin", 0), ("lineA", 1),
+    ("line_end", 2), ("lineB", 0), ("lineA", 0), ("line_end", 1), ("near", 1, 0, 1), ("line_end", 3),
+    ("near", 2, -1, -1), ("near", 2, 2, -1), ("near", 1, 1, -1), ("near", 2, -1, 1), ("near", 3, 1, -1),
+    ("line_end", 0), ("near", 2, 2, 1), ("unpack", 2, 0), ("near", 1, 0, -1), ("near", 0, 1, 1), ("near", 2, 0, 1),
+    ("near", 2, 1, -1), ("near", 1, 2, 1), ("near", 1, -1, -1), ("near", 1, -1, 1), ("near", 2, 1, 1),
+    ("near", 2, 0, -1), ("near", 3, -1, 1), ("near", 3, 0, -1), ("near", 1, 2, -1), ("near", 1, 1, 1),
+    ("unpack", 1, 1), ("near", 0, -1, -1), ("unpack", 1, 0), ("near", 0, 0, -1), ("near", 3, 0, 1), ("unpack", 2, 3),
+    ("near", 3, 1, 1), ("unpack", 1, 3), ("near", 3, -1, -1), ("unpack", 0, 0), ("unpack", 2, 1), ("unpack", 3, 0),
+    ("near", 3, 2, 1), ("near", 0, 0, 1), ("near", 0, 1, -1), ("near", 0, -1, 1), ("unpack", 3, 1), ("near", 0, 2, 1),
+    ("near", 0, 2, -1), ("unpack", 0, 3), ("halves", 1), ("unpack", 0, 1), ("near", 3, 2, -1), ("far", 2),
+    ("unpack", 3, 3), ("far", 1), ("unpack", 1, 2), ("halves", 2), ("unpack", 2, 2), ("far", 0), ("far", 3),
+    ("unpack", 3, 2), ("unpack", 0, 2),
 )
 LINE = {"x": (0, 1), "z": (1, 0)}
 
 
+DIAGONAL = (0, 0)
+EXTRA = 8
+
+
 def block_rows(d):
-    return B // 2 if d in HALVES else B
+    return B // 2 if d in HALVES or d == DIAGONAL else B
 
 
 def chunk_rows(q):
     return sum(block_rows(d) for d in CHUNKS[q][1])
+
+
+def gather_rows(q):
+    return chunk_rows(q) + (EXTRA if DIAGONAL in CHUNKS[q][1] else 0)
 
 
 def offset(q, d):
@@ -69,11 +78,11 @@
     return high, (v - high.astype(f32)).astype(bf16)
 
 
-def kernel(x_hbm, shifts_hbm, orders_hbm, child_hbm, o_ref, *scratch):
+def kernel(x_hbm, shifts_hbm, orders_hbm, child_hbm, o_hbm, *scratch):
     nq = len(CHUNKS)
     pack, parts, chosen, stage = (scratch[i * nq : (i + 1) * nq] for i in range(4))
-    sh, sl, lhs, first_strip, res, ssq, scale, s1, r1, s2, r2, s3, r3 = scratch[4 * nq : 4 * nq + 13]
-    x_ref, shifts, orders, child, arg_sems = scratch[4 * nq + 13 :]
+    sh, sl, lhs, first_strip, res, ssq, scale, s1, r1, s2, r2, s3, r3, s4, r4 = scratch[4 * nq : 4 * nq + 15]
+    x_ref, shifts, orders, child, arg_sems, extra_out, extra_in, out_sems = scratch[4 * nq + 15 :]
 
     fetches = [
         pltpu.make_async_copy(src, dst, arg_sems.at[i])
@@ -114,11 +123,16 @@
         lax.broadcasted_iota(jnp.int32, (B, B), 0) == lax.broadcasted_iota(jnp.int32, (B, B), 1)
     )
 
+    half_row = lax.broadcasted_iota(jnp.int32, (B // 2, B), 0)
+    half_lane = lax.broadcasted_iota(jnp.int32, (B // 2, B), 1)
+    upper = half_row <= half_lane
+    lower_eye = half_lane == half_row + B // 2
+
     def fill(q):
         for d in CHUNKS[q][1]:
             there = lax.rem(true_z + d[0], SIDE) * SIDE + lax.rem(true_x + d[1], SIDE)
             blk = x_ref[0, :, pl.ds(pl.multiple_of(there * B, B), B)]
-            if d == (0, 0):
+            if d == DIAGONAL:
                 blk = blk - jnp.where(eye, shift, jnp.float32(0.0))
             live = jnp.maximum(col, there) * B < order
             blk = blk * jnp.where(live, jnp.float32(1.0), jnp.float32(0.0))
@@ -128,6 +142,11 @@
                 one = jnp.where(leads, jnp.float32(1.0), jnp.float32(0.0))
                 mirror = blk.T
                 pack[q][at : at + B // 2] = blk[: B // 2] * one + mirror[B // 2 :] * (1.0 - one)
+            elif d == DIAGONAL:
+                top, bottom = blk[: B // 2], blk[B // 2 :]
+                pack[q][at : at + B // 2] = jnp.where(upper, top, pltpu.roll(bottom, B // 2, 1))
+                last = jnp.sum(jnp.where(lower_eye, bottom, 0.0), axis=0, keepdims=True)
+                extra_out[...] = jnp.broadcast_to(last, (EXTRA, B))
             else:
                 pack[q][at : at + B] = blk
 
@@ -169,11 +188,33 @@
             second[q, delta] = copy
         stage[q][0, mine] = parts[q][child[row]]
 
+    fourth = {}
+
+    def extra():
+        for delta in range(1, ROWS):
+            copy = pltpu.make_async_remote_copy(
+                src_ref=extra_out,
+                dst_ref=extra_in.at[row],
+                send_sem=s4.at[delta],
+                recv_sem=r4.at[delta],
+                device_id=to_row(delta),
+                device_id_type=MESH,
+            )
+            copy.start()
+            fourth[delta] = copy
+        extra_in[row] = extra_out[...]
+
+    def take():
+        for delta in range(1, ROWS):
+            fourth[delta].wait_recv()
+        stage[0][0, chunk_rows(0) :] = extra_in[child[row]]
+
     third = {}
 
     def send(q, r, half, e, sign):
-        n = chunk_rows(q)
-        rows = {"all": pl.ds(0, n), "top": pl.ds(0, n // 2), "low": pl.ds(n // 2, n // 2)}[half]
+        n = gather_rows(q)
+        cut = (n // 2 + 7) // 8 * 8
+        rows = {"all": pl.ds(0, n), "top": pl.ds(0, cut), "low": pl.ds(cut, n - cut)}[half]
         lands = plus(r, e, -sign)
         slot = (q * STRIPS + flat(lands)) * 2 + (1 if half == "low" else 0)
         copy = pltpu.make_async_remote_copy(
@@ -222,6 +263,17 @@
     def square(blk, weight):
         ssq[...] += weight * jnp.sum((blk * blk).reshape(-1, 8, B), axis=0)
 
+    def diagonal(part, last):
+        mirror = jnp.concatenate([part, jnp.zeros_like(part)], axis=0).T
+        above = mirror[: B // 2]
+        top = jnp.where(upper, part, above)
+        right = jnp.where(
+            half_lane < half_row + B // 2, pltpu.roll(part, B // 2, 1), pltpu.roll(above, B // 2, 1)
+        )
+        right = jnp.where(lower_eye, last, right)
+        bottom = jnp.where(half_lane < B // 2, mirror[B // 2 :], right)
+        return jnp.concatenate([top, bottom], axis=0)
+
     def unpack(q, k):
         if all(d in HALVES for d in CHUNKS[q][1]):
             return
@@ -234,11 +286,12 @@
                 if d in HALVES:
                     continue
                 at = offset(q, d)
-                blk = stage[q][r, at : at + B]
-                if d == (0, 0):
+                if d == DIAGONAL:
+                    blk = diagonal(stage[q][r, at : at + B // 2], stage[q][r, chunk_rows(q) :][0:1])
                     square(blk, 1.0)
                     put(r, r, blk)
                 else:
+                    blk = stage[q][r, at : at + B]
                     square(blk, 2.0)
                     dz, dx = d[0] + (d[1] - d[0]) * turned, d[1] + (d[0] - d[1]) * turned
                     put(r, lax.rem(rz + dz, SIDE) * SIDE + lax.rem(rx + dx, SIDE), blk)
@@ -314,6 +367,8 @@
         "fill": fill,
         "spread": spread,
         "choose": choose,
+        "extra": lambda _: extra(),
+        "take": lambda _: take(),
         "begin": begin_gather,
         "lineA": line_a,
         "lineB": line_b,
@@ -335,15 +390,17 @@
     total = jnp.sum(jnp.sum(ssq[...], axis=0, keepdims=True), axis=1, keepdims=True)
     scale[...] = root / (2.0 * jnp.sqrt(jnp.broadcast_to(total, (1, M)) + 1e-06))
 
-    def load(k, v):
+    def load(k, v, cs=slice(None)):
         high, low = split(v)
-        lhs[k, 0:B] = high
-        lhs[k, B : 2 * B] = low
-
-    def product(k):
-        both = jnp.dot(lhs[k], sh[...], preferred_element_type=f32)
-        low = jnp.dot(lhs[k, 0:B], sl[...], preferred_element_type=f32)
-        return (both[0:B] + both[B : 2 * B] + low) * scale[...]
+        lhs[k, 0:B, cs] = high
+        lhs[k, B : 2 * B, cs] = low
+
+    def quarter(k, cs):
+        both = jnp.dot(lhs[k], sh[:, cs], preferred_element_type=f32)
+        low = jnp.dot(lhs[k, 0:B], sl[:, cs], preferred_element_type=f32)
+        return (both[0:B] + both[B : 2 * B] + low) * scale[:, cs]
+
+    spans = [pl.ds(j * SPAN, SPAN) for j in range(SIDE)]
 
     own = (sh[0:B].astype(f32) + sl[0:B].astype(f32)) * scale[...]
     first_strip[...] = own
@@ -355,28 +412,36 @@
         keep = jnp.where(begins, jnp.float32(1.5), jnp.float32(0.0))
         take = jnp.where(begins, jnp.float32(-0.5), jnp.float32(1.0))
         weight = jnp.where(
-            begins,
-            jnp.float32(1.5),
-            jnp.where(
-                m == 1, jnp.float32(-1.125), jnp.where(m == 2, jnp.float32(0.75), jnp.float32(-0.125))
-            ),
+            begins, jnp.float32(1.5), jnp.where(m == 1, jnp.float32(-1.125), jnp.float32(0.75))
         )
-        load(1, product(0))
-        v = keep * first_strip[...] + take * product(1)
-        res[...] += weight * v
-        load(0, v)
+        for cs in spans:
+            load(1, quarter(0, cs), cs)
+        for cs in spans:
+            v = keep * first_strip[:, cs] + take * quarter(1, cs)
+            res[:, cs] += weight * v
+            load(0, v, cs)
         return 0
 
-    lax.fori_loop(0, 4, twice, 0)
-
-    for rz in range(SIDE):
+    lax.fori_loop(0, 3, twice, 0)
+
+    for cs in spans:
+        load(1, quarter(0, cs), cs)
+    leaving = []
+    for j, cs in enumerate(spans):
+        res[:, cs] = (res[:, cs] - 0.125 * quarter(1, cs)) * root[:, 0:SPAN]
         for rx in range(SIDE):
-            r = flat((rz, rx))
-            o_ref[0, :, pl.ds(pl.multiple_of(place((rz, rx)) * B, B), B)] = (
-                res[:, r * B : (r + 1) * B] * root[:, 0:B]
+            r = flat((j, rx))
+            copy = pltpu.make_async_copy(
+                res.at[:, pl.ds(r * B, B)],
+                o_hbm.at[0, :, pl.ds(pl.multiple_of(place((j, rx)) * B, B), B)],
+                out_sems.at[r],
             )
-
-    for copies in (first, second, third):
+            copy.start()
+            leaving.append(copy)
+    for copy in leaving:
+        copy.wait()
+
+    for copies in (first, second, third, fourth):
         for copy in copies.values():
             copy.wait_send()
 
@@ -389,11 +454,11 @@
         kernel,
         out_shape=jax.ShapeDtypeStruct(parent_blocks.shape, f32),
         in_specs=[anywhere] * 4,
-        out_specs=pl.BlockSpec(memory_space=pltpu.VMEM),
+        out_specs=anywhere,
         scratch_shapes=[pltpu.VMEM((n, B), f32) for n in rows]
         + [pltpu.VMEM((ROWS, n // ROWS, B), f32) for n in rows]
         + [pltpu.VMEM((ROWS, n // ROWS, B), f32) for n in rows]
-        + [pltpu.VMEM((STRIPS, n, B), f32) for n in rows]
+        + [pltpu.VMEM((STRIPS, gather_rows(q), B), f32) for q in range(nq)]
         + [
             pltpu.VMEM((M, M), bf16),
             pltpu.VMEM((M, M), bf16),
@@ -408,11 +473,16 @@
             pltpu.SemaphoreType.DMA((nq * ROWS,)),
             pltpu.SemaphoreType.DMA((nq * STRIPS * 2,)),
             pltpu.SemaphoreType.DMA((nq * STRIPS * 2,)),
+            pltpu.SemaphoreType.DMA((ROWS,)),
+            pltpu.SemaphoreType.DMA((ROWS,)),
             pltpu.VMEM(parent_blocks.shape, f32),
             pltpu.SMEM(shifts.shape, f32),
             pltpu.SMEM(orders.shape, jnp.int32),
             pltpu.SMEM(child_order.shape, jnp.int32),
             pltpu.SemaphoreType.DMA((4,)),
+            pltpu.VMEM((EXTRA, B), f32),
+            pltpu.VMEM((ROWS, EXTRA, B), f32),
+            pltpu.SemaphoreType.DMA((STRIPS,)),
         ],
         compiler_params=pltpu.CompilerParams(
             collective_id=0, has_side_effects=True, vmem_limit_bytes=60 * 2**20

time: 100 us -> 97.4 us (0.974)
  Pallas kernels: 97.8 us -> 94.9 us
    pallas_call x1, Pallas kernels: 97.8 us -> 94.9 us  [local(): pl.pallas_call(kernel, out_shape=jax.ShapeDtypeStruct(parent_blocks.shape...]
where the time goes in v4:
time: 97.4 us; the launch traced here: 97.2 us
  Pallas kernels  94.9 us (97%)
  local copies, waits for them, and re-layouts  2.3 us (2%)
    pallas_call x1, Pallas kernels, local(): pl.pallas_call(kernel, out_shape=jax.ShapeDtypeStruct(parent_blocks.shape...  94.9 us
    unnamed x1, local copies, waits for them, and re-layouts  2.3 us

profile of v4, /device:TPU:1, one launch (start us, length us, event | category | flops | bytes accessed | tf_op | source)
XLA Modules:
  0.0 97.2 jit_solution(11433864370459923941)
XLA Ops:
  0.0 94.9 %sign_steps.1 = f32[1,128,2048]{2,1,0:T(8,128)} custom-call(f32[1,128,2048]{2,1,0:T(8,128)} %x_hbm.1, f32[8]{0:T(128)} %shifts_hbm.1, s32[8]{0:T(128)} %orders_hbm.1, s32[8]{0:T(128)} %child_hbm.1), custom_call_target="tpu_custom_call" | custom-call | flops 25769803776 | bytes 2097152 | tf_op jit(solution)/shard_map/sign_steps/pallas_call | solution.py:453
  94.9 2.3 %copy.6 = f32[1,128,2048]{2,1,0:T(8,128)} copy(f32[1,128,2048]{2,1,0:T(8,128)} %sign_steps.1) | data formatting | bytes 2097152

commit v5 on v4

--- a/solution.py
+++ b/solution.py
@@ -81,8 +81,8 @@
 def kernel(x_hbm, shifts_hbm, orders_hbm, child_hbm, o_hbm, *scratch):
     nq = len(CHUNKS)
     pack, parts, chosen, stage = (scratch[i * nq : (i + 1) * nq] for i in range(4))
-    sh, sl, lhs, first_strip, res, ssq, scale, s1, r1, s2, r2, s3, r3, s4, r4 = scratch[4 * nq : 4 * nq + 15]
-    x_ref, shifts, orders, child, arg_sems, extra_out, extra_in, out_sems = scratch[4 * nq + 15 :]
+    sh, sl, lhs, strip, ssq, scale, s1, r1, s2, r2, s3, r3, s4, r4 = scratch[4 * nq : 4 * nq + 14]
+    x_ref, shifts, orders, child, arg_sems, extra_out, extra_in, out_sems = scratch[4 * nq + 14 :]
 
     fetches = [
         pltpu.make_async_copy(src, dst, arg_sems.at[i])
@@ -402,37 +402,37 @@
 
     spans = [pl.ds(j * SPAN, SPAN) for j in range(SIDE)]
 
-    own = (sh[0:B].astype(f32) + sl[0:B].astype(f32)) * scale[...]
-    first_strip[...] = own
-    res[...] = jnp.zeros_like(res)
-    load(0, own)
-
-    def twice(m, _):
-        begins = m == 0
-        keep = jnp.where(begins, jnp.float32(1.5), jnp.float32(0.0))
-        take = jnp.where(begins, jnp.float32(-0.5), jnp.float32(1.0))
-        weight = jnp.where(
-            begins, jnp.float32(1.5), jnp.where(m == 1, jnp.float32(-1.125), jnp.float32(0.75))
-        )
+    for cs in spans:
+        own = (sh[0:B, cs].astype(f32) + sl[0:B, cs].astype(f32)) * scale[:, cs]
+        strip[:, cs] = own
+        load(0, own, cs)
+
+    for cs in spans:
+        load(1, quarter(0, cs), cs)
+    for cs in spans:
+        v = 1.5 * strip[:, cs] - 0.5 * quarter(1, cs)
+        strip[:, cs] = v
+        load(0, -0.125 * v, cs)
+
+    def horner(m, _):
+        weight = jnp.where(m == 0, jnp.float32(0.75), jnp.float32(-1.125))
         for cs in spans:
             load(1, quarter(0, cs), cs)
         for cs in spans:
-            v = keep * first_strip[:, cs] + take * quarter(1, cs)
-            res[:, cs] += weight * v
-            load(0, v, cs)
+            load(0, quarter(1, cs) + weight * strip[:, cs], cs)
         return 0
 
-    lax.fori_loop(0, 3, twice, 0)
+    lax.fori_loop(0, 2, horner, 0)
 
     for cs in spans:
         load(1, quarter(0, cs), cs)
     leaving = []
     for j, cs in enumerate(spans):
-        res[:, cs] = (res[:, cs] - 0.125 * quarter(1, cs)) * root[:, 0:SPAN]
+        strip[:, cs] = (quarter(1, cs) + 1.5 * strip[:, cs]) * root[:, 0:SPAN]
         for rx in range(SIDE):
             r = flat((j, rx))
             copy = pltpu.make_async_copy(
-                res.at[:, pl.ds(r * B, B)],
+                strip.at[:, pl.ds(r * B, B)],
                 o_hbm.at[0, :, pl.ds(pl.multiple_of(place((j, rx)) * B, B), B)],
                 out_sems.at[r],
             )
@@ -463,7 +463,6 @@
             pltpu.VMEM((M, M), bf16),
             pltpu.VMEM((M, M), bf16),
             pltpu.VMEM((2, 2 * B, M), bf16),
-            pltpu.VMEM((B, M), f32),
             pltpu.VMEM((B, M), f32),
             pltpu.VMEM((8, B), f32),
             pltpu.VMEM((1, M), f32),

time: 97.4 us -> 96.7 us (level)
  no operation moved by 1% of the time
where the time goes in v5:
time: 96.7 us; the launch traced here: 96.5 us
  Pallas kernels  94.2 us (97%)
  local copies, waits for them, and re-layouts  2.3 us (2%)
    pallas_call x1, Pallas kernels, local(): pl.pallas_call(kernel, out_shape=jax.ShapeDtypeStruct(parent_blocks.shape...  94.2 us
    unnamed x1, local copies, waits for them, and re-layouts  2.3 us

profile of v5, /device:TPU:1, one launch (start us, length us, event | category | flops | bytes accessed | tf_op | source)
XLA Modules:
  0.0 96.5 jit_solution(1766492429431712824)
XLA Ops:
  0.0 94.2 %sign_steps.1 = f32[1,128,2048]{2,1,0:T(8,128)} custom-call(f32[1,128,2048]{2,1,0:T(8,128)} %x_hbm.1, f32[8]{0:T(128)} %shifts_hbm.1, s32[8]{0:T(128)} %orders_hbm.1, s32[8]{0:T(128)} %child_hbm.1), custom_call_target="tpu_custom_call" | custom-call | flops 25769803776 | bytes 2097152 | tf_op jit(solution)/shard_map/sign_steps/pallas_call | solution.py:453
  94.2 2.3 %copy.6 = f32[1,128,2048]{2,1,0:T(8,128)} copy(f32[1,128,2048]{2,1,0:T(8,128)} %sign_steps.1) | data formatting | bytes 2097152

commit v6 on v5

--- a/solution.py
+++ b/solution.py
@@ -23,20 +23,20 @@
     ("z", ((1, 2), (1, 3))),
 )
 ORDER = (
-    ("fill", 3), ("spread", 3), ("fill", 1), ("fill", 2), ("spread", 2), ("spread", 1), ("choose", 3), ("choose", 2),
-    ("choose", 1), ("begin", 3), ("fill", 0), ("spread", 0), ("begin", 2), ("begin", 1), ("lineB", 3), ("choose", 0),
-    ("lineA", 3), ("lineB", 2), ("lineB", 1), ("extra", 0), ("lineA", 2), ("take", 0), ("begin", 0), ("lineA", 1),
-    ("line_end", 2), ("lineB", 0), ("lineA", 0), ("line_end", 1), ("near", 1, 0, 1), ("line_end", 3),
-    ("near", 2, -1, -1), ("near", 2, 2, -1), ("near", 1, 1, -1), ("near", 2, -1, 1), ("near", 3, 1, -1),
-    ("line_end", 0), ("near", 2, 2, 1), ("unpack", 2, 0), ("near", 1, 0, -1), ("near", 0, 1, 1), ("near", 2, 0, 1),
-    ("near", 2, 1, -1), ("near", 1, 2, 1), ("near", 1, -1, -1), ("near", 1, -1, 1), ("near", 2, 1, 1),
-    ("near", 2, 0, -1), ("near", 3, -1, 1), ("near", 3, 0, -1), ("near", 1, 2, -1), ("near", 1, 1, 1),
-    ("unpack", 1, 1), ("near", 0, -1, -1), ("unpack", 1, 0), ("near", 0, 0, -1), ("near", 3, 0, 1), ("unpack", 2, 3),
-    ("near", 3, 1, 1), ("unpack", 1, 3), ("near", 3, -1, -1), ("unpack", 0, 0), ("unpack", 2, 1), ("unpack", 3, 0),
-    ("near", 3, 2, 1), ("near", 0, 0, 1), ("near", 0, 1, -1), ("near", 0, -1, 1), ("unpack", 3, 1), ("near", 0, 2, 1),
-    ("near", 0, 2, -1), ("unpack", 0, 3), ("halves", 1), ("unpack", 0, 1), ("near", 3, 2, -1), ("far", 2),
-    ("unpack", 3, 3), ("far", 1), ("unpack", 1, 2), ("halves", 2), ("unpack", 2, 2), ("far", 0), ("far", 3),
-    ("unpack", 3, 2), ("unpack", 0, 2),
+    ("fill", 0), ("spread", 0), ("fill", 1), ("spread", 1), ("fill", 2), ("extra", 0), ("spread", 2), ("choose", 0),
+    ("choose", 1), ("fill", 3), ("spread", 3), ("take", 0), ("begin", 0), ("choose", 2), ("begin", 1), ("lineA", 0),
+    ("begin", 2), ("lineB", 0), ("choose", 3), ("lineB", 1), ("lineA", 1), ("begin", 3), ("near", 0, 0, 1),
+    ("lineA", 2), ("near", 1, -1, 1), ("near", 1, -1, -1), ("line_end", 1), ("lineB", 3), ("lineA", 3),
+    ("unpack", 1, 0), ("line_end", 0), ("near", 0, 0, -1), ("near", 1, 0, -1), ("lineB", 2), ("near", 1, 2, 1),
+    ("near", 0, 1, -1), ("line_end", 3), ("near", 1, 1, -1), ("near", 1, 1, 1), ("near", 1, 0, 1), ("near", 1, 2, -1),
+    ("near", 0, 2, -1), ("unpack", 1, 1), ("near", 0, -1, 1), ("near", 3, 0, 1), ("near", 0, 1, 1), ("unpack", 0, 0),
+    ("near", 0, 2, 1), ("near", 3, 0, -1), ("near", 0, -1, -1), ("line_end", 2), ("unpack", 3, 0),
+    ("near", 3, -1, -1), ("near", 2, -1, -1), ("near", 2, 0, 1), ("unpack", 1, 3), ("unpack", 2, 0),
+    ("near", 2, -1, 1), ("unpack", 0, 3), ("near", 3, -1, 1), ("near", 2, 1, 1), ("near", 2, 0, -1),
+    ("near", 3, 1, 1), ("unpack", 0, 1), ("halves", 1), ("near", 3, 2, 1), ("near", 2, 1, -1), ("near", 3, 2, -1),
+    ("unpack", 3, 1), ("near", 3, 1, -1), ("far", 0), ("near", 2, 2, -1), ("unpack", 0, 2), ("near", 2, 2, 1),
+    ("unpack", 2, 3), ("far", 1), ("unpack", 1, 2), ("unpack", 3, 3), ("halves", 2), ("unpack", 2, 1), ("far", 2),
+    ("unpack", 2, 2), ("far", 3), ("unpack", 3, 2),
 )
 LINE = {"x": (0, 1), "z": (1, 0)}
 

time: 96.7 us -> 95.8 us (level)
  no operation moved by 1% of the time
where the time goes in v6:
time: 95.8 us; the launch traced here: 95.6 us
  Pallas kernels  93.3 us (97%)
  local copies, waits for them, and re-layouts  2.3 us (2%)
    pallas_call x1, Pallas kernels, local(): pl.pallas_call(kernel, out_shape=jax.ShapeDtypeStruct(parent_blocks.shape...  93.3 us
    unnamed x1, local copies, waits for them, and re-layouts  2.3 us

profile of v6, /device:TPU:1, one launch (start us, length us, event | category | flops | bytes accessed | tf_op | source)
XLA Modules:
  0.0 95.6 jit_solution(6380953364715874177)
XLA Ops:
  0.0 93.3 %sign_steps.1 = f32[1,128,2048]{2,1,0:T(8,128)} custom-call(f32[1,128,2048]{2,1,0:T(8,128)} %x_hbm.1, f32[8]{0:T(128)} %shifts_hbm.1, s32[8]{0:T(128)} %orders_hbm.1, s32[8]{0:T(128)} %child_hbm.1), custom_call_target="tpu_custom_call" | custom-call | flops 25769803776 | bytes 2097152 | tf_op jit(solution)/shard_map/sign_steps/pallas_call | solution.py:453
  93.3 2.3 %copy.6 = f32[1,128,2048]{2,1,0:T(8,128)} copy(f32[1,128,2048]{2,1,0:T(8,128)} %sign_steps.1) | data formatting | bytes 2097152
